TPU v7x, 256 devices: a whole 4x4x8 slice. The times are simulated.
256 devices in a mesh: seq: 64 (over z_lo, x, y), head: 4 (over z_hi, core).
Axes of the slice: x: 4, y: 4, z: 8 (z_hi: 2, z_lo: 4; z = z_hi * 4 + z_lo), core: 2. Of those that a mesh axis runs over, the one named last changes fastest.
Arguments:
- tile_query: bfloat16 [768, 32768], P('head', 'seq')
- tile_key: bfloat16 [768, 32768], P('head', 'seq')
- tile_value: bfloat16 [768, 32768], P('head', 'seq'), may hold values from -6 to 6
- out_cotangent: bfloat16 [768, 32768], P('head', 'seq'), may hold values from -6 to 6
Outputs:
- attended: bfloat16 [768, 32768], P('head', 'seq')
- grad_query: bfloat16 [768, 32768], P('head', 'seq')
- grad_key: bfloat16 [768, 32768], P('head', 'seq')
- grad_value: bfloat16 [768, 32768], P('head', 'seq')
All inputs are finite; a program needn't handle non-finite values.
Results may differ from a plain program's by a relative error of at most 0.023.
Values may be sent and summed in bfloat16 or wider, within the bound.
A program may use at most 192 MiB of HBM per device.

v0:
```python
import math

import jax
import jax.numpy as jnp
from jax import lax
from jax.experimental import pallas as pl
from jax.experimental.pallas import tpu as pltpu
from jax.sharding import PartitionSpec as P

E = 64
HEADS = 3
N = 512
W = HEADS * 128
F32 = jnp.float32
BF16 = jnp.bfloat16
NEG = -1e30
SCALE2 = math.log2(math.e) / math.sqrt(E)

Y0, X0, Z0, RROWS = 0, 512, 1024, 1536
Y_AT = {1: 0, 2: 256, 3: 384}
Y_ROWS = {1: 256, 2: 128, 3: 128}
X_AT = {4: 512, 8: 768, 12: 896}
X_ROWS = {4: 64, 8: 32, 12: 32}


def nn(a, b):
    return lax.dot_general(a, b, (((1,), (0,)), ((), ())), preferred_element_type=F32)


def nt(a, b):
    return lax.dot_general(a, b, (((1,), (1,)), ((), ())), preferred_element_type=F32)


def level_of(index):
    level = jnp.zeros(index.shape, jnp.int32)
    for bound in (8, 16, 32, 64, 128, 256):
        level = level + (index < bound).astype(jnp.int32)
    return level


def pad_lanes(x, value, lanes=N):
    if x.shape[1] == lanes:
        return x
    fill = jnp.full((x.shape[0], lanes - x.shape[1]), value, x.dtype)
    return jnp.concatenate([x, fill], axis=1)


def body(
    q_hbm, k_hbm, v_hbm, c_hbm, o_hbm, gq_hbm, gk_hbm, gv_hbm,
    xin, pt, own, d6, qc, xp, rq, rc, bias0, bias1, bias2,
    e0, dp0, e1, e2, num, dqa,
    rk, rkt, t32, t48, gsend, yacc, pacc, oacc, rx, rz, ry, ryz, rzz,
    ov, gqv, gkv, gvv,
    in_sem, out_sem, send_sem, recv_sem,
):
    me = lax.axis_index("seq")
    head0 = lax.axis_index("head") * HEADS
    z, x, y = lax.div(me, 16), lax.rem(lax.div(me, 4), 4), lax.rem(me, 4)

    def flipped(v, bits):
        if bits == 0:
            return v
        if bits == 1:
            return v + 1 - 2 * lax.rem(v, 2)
        if bits == 2:
            return lax.rem(v + 2, 4)
        return 3 - v

    peer = {e: flipped(z, e // 16) * 16 + flipped(x, e // 4 % 4) * 4 + flipped(y, e % 4)
            for e in (1, 2, 3, 4, 8, 12, 16, 32, 48)}

    loads = []
    for at, src in enumerate((k_hbm, v_hbm, q_hbm, c_hbm)):
        load = pltpu.make_async_copy(src, xin.at[:, pl.ds(64 * at, 64), :], in_sem.at[at])
        load.start()
        loads.append(load)
    barrier = pltpu.get_barrier_semaphore()
    for e in peer:
        pl.semaphore_signal(
            barrier, inc=1, device_id={"seq": peer[e]}, device_id_type=pl.DeviceIdType.MESH
        )

    started = []

    def send(src, dst, e):
        at = len(started)
        copy = pltpu.make_async_remote_copy(
            src_ref=src,
            dst_ref=dst,
            send_sem=send_sem.at[at],
            recv_sem=recv_sem.at[at],
            device_id={"seq": peer[e]},
            device_id_type=pl.DeviceIdType.MESH,
        )
        copy.start()
        started.append(copy)
        return copy

    place = lax.broadcasted_iota(jnp.int32, (N, 128), 0)
    lane = lax.broadcasted_iota(jnp.int32, (8, 128), 1)
    u = 64 * place
    for bits in range(4, 10):
        u = jnp.where(place >= 1 << (bits - 1), ((2 * place + 1) << (9 - bits)) & (N - 1), u)
    for h in range(HEADS):
        for t in range(4):
            tile = (lane + (128 * t + N) - (head0 + h)) & (N - 1)
            hot = u == jnp.broadcast_to(tile[0:1], (N, 128))
            pt[h, :, 128 * t : 128 * t + 128] = jnp.where(hot, 1.0, 0.0).astype(BF16)

    for load in loads:
        load.wait()
    low = lax.broadcasted_iota(jnp.int32, (N, 128), 1) < E
    for h in range(HEADS):
        hs = slice(128 * h, 128 * h + 128)
        rows = nt(pt[h], xin[h])
        own[:, hs] = rows[:, 0:128].astype(BF16)
        d6[:, hs] = jnp.concatenate([rows[0:8, 0:128]] * 2, axis=0).astype(BF16)
        right = rows[:, 128:256]
        qc[h, 0:N, :] = jnp.where(low, right, 0.0).astype(BF16)
        qc[h, N : 2 * N, :] = jnp.where(low, 0.0, right).astype(BF16)

    pl.semaphore_wait(barrier, len(peer))
    first = {}
    first[4] = send(own.at[0:64], rk.at[512:576], 4)
    first[8] = send(own.at[0:32], rk.at[768:800], 8)
    first[12] = send(own.at[0:32], rk.at[896:928], 12)
    first[16] = send(own.at[0:16], rk.at[1024:1040], 16)
    first[32] = send(d6, t32, 32)
    first[48] = send(d6, t48, 48)
    for e in (1, 2, 3):
        first[e] = send(own.at[0 : Y_ROWS[e]], rk.at[Y_AT[e] : Y_AT[e] + Y_ROWS[e]], e)

    def fill_bias(ref, at, rows, lanes, key_place, group):
        lq = level_of(lax.broadcasted_iota(jnp.int32, (rows, lanes), 1))
        mult = jnp.minimum(lq, level_of(key_place)) - (group - 1)
        value = jnp.where(mult > 0, jnp.log2(jnp.maximum(mult, 1).astype(F32)), NEG)
        ref[at : at + rows, :] = value

    r256 = lax.broadcasted_iota(jnp.int32, (256, 256), 0)
    fill_bias(bias0, 0, 256, 256, r256, 0)
    fill_bias(bias1, 0, 256, 256, r256, 1)
    r256 = lax.broadcasted_iota(jnp.int32, (256, 128), 0)
    fill_bias(bias2, 0, 256, 128, r256 & 127, 2)
    fill_bias(bias2, 256, 256, 128, r256 & 63, 3)
    fill_bias(bias2, 512, 256, 128, r256 & 31, 4)
    r512 = lax.broadcasted_iota(jnp.int32, (512, 128), 0)
    in_pack = r512 & 31
    fill_bias(
        bias2, 768, 512, 128, jnp.where(in_pack < 16, in_pack, 0), jnp.where(in_pack < 16, 5, 6)
    )

    zero = jnp.zeros((E, N), BF16)
    for h in range(HEADS):
        cols = nt(xin[h], pt[h]).astype(BF16)
        xp[h] = cols
        rq[h, 0:E, :] = cols[128:192]
        rq[h, E:128, :] = zero
        rc[h, 0:E, :] = zero
        rc[h, E:128, :] = cols[192:256]

    def attend(keys, queries, bias_value):
        score = nn(keys, queries) * SCALE2
        if bias_value is not None:
            score = score + bias_value
        peak = jnp.max(score, axis=0, keepdims=True)
        expo = jnp.exp2(score - peak)
        return peak, expo, jnp.sum(expo, axis=0, keepdims=True)

    peaks = [[] for _ in range(HEADS)]
    sums = [[] for _ in range(HEADS)]

    def local_forward(h):
        hs = slice(128 * h, 128 * h + 128)
        pieces = []
        for t in range(2):
            qs = slice(256 * t, 256 * t + 256)
            score = nn(own[:, hs], rq[h, :, qs]) * SCALE2
            if t == 0:
                score = jnp.concatenate([score[0:256] + bias0[...], score[256:512]], axis=0)
            peak = jnp.max(score, axis=0, keepdims=True)
            expo = jnp.exp2(score - peak)
            e0[h, :, qs] = expo
            num[h, :, qs] = nn(xp[h, 0:128, :], expo.astype(BF16))
            pieces.append((peak, jnp.sum(expo, axis=0, keepdims=True)))
        peaks[h].append(jnp.concatenate([p for p, _ in pieces], axis=1))
        sums[h].append(jnp.concatenate([s for _, s in pieces], axis=1))
        dp0[h] = nn(own[:, hs], rc[h])

    local_forward(0)

    for e in (16, 32, 48):
        first[e].wait_recv()
    rk[Z0 + 16 : Z0 + 32, :] = jnp.concatenate(
        [t32[...].astype(F32)[0:8], t48[...].astype(F32)[8:16]], axis=0
    ).astype(BF16)
    packs = {}
    for e in (1, 2, 3, 4, 8, 12):
        packs[e] = send(rk.at[Z0 : Z0 + 32], rk.at[Z0 + 32 * e : Z0 + 32 * e + 32], e)
    second = []
    for b in (1, 2, 3):
        first[b].wait_recv()
        for e in (4, 8, 12):
            n = X_ROWS[e]
            to = X_AT[e] + n * b
            second.append(send(rk.at[Y_AT[b] : Y_AT[b] + n], rk.at[to : to + n], e))

    local_forward(1)
    for b in (1, 2, 3):
        packs[b].wait_recv()
    for e in (4, 8, 12):
        to = Z0 + 32 * e + 32
        second.append(send(rk.at[Z0 + 32 : Z0 + 128], rk.at[to : to + 96], e))

    local_forward(2)

    nums1 = []
    nums2 = []
    for h in range(HEADS):
        hs = slice(128 * h, 128 * h + 128)
        rkt[h, :, 0:512] = rk[0:512, hs].T
        peak, expo, total = attend(rk[0:256, hs], rq[h, :, 0:256], bias1[...])
        e1[h] = expo
        nums1.append(nn(rkt[h, :, 0:256], expo.astype(BF16)))
        peaks[h].append(pad_lanes(peak, NEG))
        sums[h].append(pad_lanes(total, 0.0))

    for e in (4, 8, 12):
        first[e].wait_recv()
        packs[e].wait_recv()
    for copy in second:
        copy.wait_recv()

    delta = []
    gain = []
    for h in range(HEADS):
        hs = slice(128 * h, 128 * h + 128)
        rkt[h, :, 512:1536] = rk[512:1536, hs].T
        peak, expo, total = attend(rk[256:1536, hs], rq[h, :, 0:128], bias2[...])
        e2[h] = expo
        nums2.append(nn(rkt[h, :, 256:1536], expo.astype(BF16)))
        peaks[h].append(pad_lanes(peak, NEG))
        sums[h].append(pad_lanes(total, 0.0))

    for h in range(HEADS):
        top = jnp.maximum(jnp.maximum(peaks[h][0], peaks[h][1]), peaks[h][2])
        factor = [jnp.exp2(p - top) for p in peaks[h]]
        norm = sum(f * s for f, s in zip(factor, sums[h]))
        inv = 1.0 / norm
        gains = [f * inv for f in factor]
        mixed = (
            num[h] * gains[0]
            + pad_lanes(nums1[h] * gains[1][:, 0:256], 0.0)
            + pad_lanes(nums2[h] * gains[2][:, 0:128], 0.0)
        )
        attended = mixed[E:128].astype(BF16)
        cot = xp[h, 192:256, :].astype(F32)
        delta.append(jnp.sum(cot * attended.astype(F32), axis=0, keepdims=True))
        gain.append(gains)
        xp[h, 192:256, :] = attended

    def backward(h, keys, dprob, expo, g, nq):
        probs = expo * g[:, 0:nq]
        if dprob is None:
            dprob = nn(keys, rc[h, :, 0:nq])
        dscore = (probs * (dprob - delta[h][:, 0:nq])).astype(BF16)
        both = jnp.concatenate([dscore, probs.astype(BF16)], axis=1)
        right = jnp.concatenate([qc[h, 0:nq, :], qc[h, N : N + nq, :]], axis=0)
        return dscore, nn(both, right)

    for h in range(HEADS):
        hs = slice(128 * h, 128 * h + 128)
        dscore, dkv = backward(h, rk[512:1536, hs], None, e2[h, 256:1280, :], gain[h][2], 128)
        gsend[512:1024, hs] = dkv[0:512].astype(BF16)
        gsend[1152:1536, hs] = dkv[640:1024].astype(BF16)
        pacc[:, hs] = dkv[512:640]
        dqa[h, :, 0:128] = nn(rkt[h, :, 512:1536], dscore)
        dqa[h, :, 128:512] = jnp.zeros((128, 384), F32)
    hop_x = {}
    rx_at = {4: 0, 8: 256, 12: 384}
    rz_at = {4: 0, 8: 128, 12: 256}
    for e in (4, 8, 12):
        n = 4 * X_ROWS[e]
        hop_x[e] = (
            send(gsend.at[X_AT[e] : X_AT[e] + n], rx.at[rx_at[e] : rx_at[e] + n], e),
            send(gsend.at[Z0 + 32 * e : Z0 + 32 * e + 128], rz.at[rz_at[e] : rz_at[e] + 128], e),
        )

    for h in range(HEADS):
        hs = slice(128 * h, 128 * h + 128)
        dscore, dkv = backward(h, rk[0:256, hs], None, e1[h], gain[h][1], 256)
        dqa[h, :, 0:256] += nn(rkt[h, :, 0:256], dscore)
        yacc[0:64, hs] = dkv[0:64]
        gsend[64:256, hs] = dkv[64:256].astype(BF16)
        dscore, dkv = backward(h, rk[256:512, hs], None, e2[h, 0:256, :], gain[h][2], 128)
        dqa[h, :, 0:128] += nn(rkt[h, :, 256:512], dscore)
        yacc[64:128, hs] = dkv[0:64]
        gsend[320:384, hs] = dkv[64:128].astype(BF16)
        yacc[128:192, hs] = dkv[128:192]
        gsend[448:512, hs] = dkv[192:256].astype(BF16)
    ry_at = {1: 0, 2: 256, 3: 384}
    tails = []
    for e in (1, 2, 3):
        n = Y_ROWS[e] - 64
        a = Y_AT[e] + 64
        b = ry_at[e] + 64
        tails.append(send(gsend.at[a : a + n], ry.at[b : b + n], e))

    def local_backward(h):
        hs = slice(128 * h, 128 * h + 128)
        dscore, dkv = backward(h, None, dp0[h], e0[h], gain[h][0], N)
        oacc[:, hs] = dkv
        dqa[h] += nn(xp[h, 0:128, :], dscore)
        both = jnp.concatenate([xp[h, 192:256, :], dqa[h, 0:E, :].astype(BF16)], axis=0)
        done = nn(both, pt[h])
        ov[h] = done[0:E].astype(BF16)
        gqv[h] = (done[E:128] * 0.125).astype(BF16)

    local_backward(0)

    for e in (4, 8, 12):
        for copy in hop_x[e]:
            copy.wait_recv()
    heads_y = []
    packs_y = []
    for b in (1, 2, 3):
        part = yacc[64 * (b - 1) : 64 * b, :] + rx[64 * b : 64 * b + 64, :].astype(F32)
        small = rx[256 + 32 * b : 288 + 32 * b, :].astype(F32) + rx[
            384 + 32 * b : 416 + 32 * b, :
        ].astype(F32)
        gsend[Y_AT[b] : Y_AT[b] + 32, :] = (part[0:32] + small).astype(BF16)
        gsend[Y_AT[b] + 32 : Y_AT[b] + 64, :] = part[32:64].astype(BF16)
        pack = pacc[32 * b : 32 * b + 32, :]
        for e in (4, 8, 12):
            pack = pack + rz[rz_at[e] + 32 * b : rz_at[e] + 32 * b + 32, :].astype(F32)
        gsend[Z0 + 32 * b : Z0 + 32 * b + 32, :] = pack.astype(BF16)
        packs_y.append(
            send(gsend.at[Z0 + 32 * b : Z0 + 32 * b + 32], ryz.at[32 * (b - 1) : 32 * b], b)
        )
        heads_y.append(
            send(gsend.at[Y_AT[b] : Y_AT[b] + 64], ry.at[ry_at[b] : ry_at[b] + 64], b)
        )

    local_backward(1)

    for copy in packs_y:
        copy.wait_recv()
    pack = pacc[0:32, :]
    for e in (4, 8, 12):
        pack = pack + rz[rz_at[e] : rz_at[e] + 32, :].astype(F32)
    for b in (1, 2, 3):
        pack = pack + ryz[32 * (b - 1) : 32 * b, :].astype(F32)
    gsend[Z0 : Z0 + 32, :] = pack.astype(BF16)
    hop_z = [
        send(gsend.at[Z0 : Z0 + 16], rzz.at[0:16], 16),
        send(gsend.at[Z0 + 16 : Z0 + 32], rzz.at[16:32], 32),
        send(gsend.at[Z0 + 16 : Z0 + 32], rzz.at[32:48], 48),
    ]

    local_backward(2)
    stores = [
        pltpu.make_async_copy(ov, o_hbm, out_sem.at[0]),
        pltpu.make_async_copy(gqv, gq_hbm, out_sem.at[1]),
    ]
    for store in stores:
        store.start()

    for copy in tails + heads_y + hop_z:
        copy.wait_recv()
    for h in range(HEADS):
        hs = slice(128 * h, 128 * h + 128)
        a = oacc[0:64, hs] + rx[0:64, hs].astype(F32)
        for b in (1, 2, 3):
            a = a + ry[ry_at[b] : ry_at[b] + 64, hs].astype(F32)
        a32 = a[0:32] + rx[256:288, hs].astype(F32) + rx[384:416, hs].astype(F32)
        a16 = a32[0:16] + rzz[0:16, hs].astype(F32)
        a8 = a16[0:8] + rzz[16:32, hs].astype(F32)[0:8] + rzz[32:48, hs].astype(F32)[8:16]
        b128 = oacc[64:128, hs]
        for b in (1, 2, 3):
            b128 = b128 + ry[ry_at[b] + 64 : ry_at[b] + 128, hs].astype(F32)
        b256 = oacc[128:256, hs] + ry[128:256, hs].astype(F32)
        whole = jnp.concatenate(
            [a8, a16[8:16], a32[16:32], a[32:64], b128, b256, oacc[256:512, hs]], axis=0
        )
        done = nn(whole.T.astype(BF16), pt[h])
        gkv[h] = (done[0:E] * 0.125).astype(BF16)
        gvv[h] = done[E:128].astype(BF16)
    last = [
        pltpu.make_async_copy(gkv, gk_hbm, out_sem.at[2]),
        pltpu.make_async_copy(gvv, gv_hbm, out_sem.at[3]),
    ]
    for store in last:
        store.start()
    for copy in started:
        copy.wait_send()
    for store in stores + last:
        store.wait()


COPIES = 45


def per_device(tile_query, tile_key, tile_value, out_cotangent):
    shape = (HEADS, E, N)
    args = [a.reshape(shape) for a in (tile_query, tile_key, tile_value, out_cotangent)]
    vm = pltpu.VMEM
    outs = pl.pallas_call(
        body,
        out_shape=[jax.ShapeDtypeStruct(shape, BF16)] * 4,
        in_specs=[pl.BlockSpec(memory_space=pl.ANY)] * 4,
        out_specs=[pl.BlockSpec(memory_space=pl.ANY)] * 4,
        scratch_shapes=[
            vm((HEADS, 256, N), BF16),
            vm((HEADS, N, N), BF16),
            vm((N, W), BF16),
            vm((16, W), BF16),
            vm((HEADS, 2 * N, 128), BF16),
            vm((HEADS, 256, N), BF16),
            vm((HEADS, 128, N), BF16),
            vm((HEADS, 128, N), BF16),
            vm((256, 256), F32),
            vm((256, 256), F32),
            vm((1280, 128), F32),
            vm((HEADS, N, N), F32),
            vm((HEADS, N, N), F32),
            vm((HEADS, 256, 256), F32),
            vm((HEADS, 1280, 128), F32),
            vm((HEADS, 128, N), F32),
            vm((HEADS, 128, N), F32),
            vm((RROWS, W), BF16),
            vm((HEADS, 128, RROWS), BF16),
            vm((16, W), BF16),
            vm((16, W), BF16),
            vm((RROWS, W), BF16),
            vm((192, W), F32),
            vm((128, W), F32),
            vm((N, W), F32),
            vm((512, W), BF16),
            vm((384, W), BF16),
            vm((512, W), BF16),
            vm((96, W), BF16),
            vm((48, W), BF16),
            vm(shape, BF16),
            vm(shape, BF16),
            vm(shape, BF16),
            vm(shape, BF16),
            pltpu.SemaphoreType.DMA((4,)),
            pltpu.SemaphoreType.DMA((4,)),
            pltpu.SemaphoreType.DMA((COPIES,)),
            pltpu.SemaphoreType.DMA((COPIES,)),
        ],
        compiler_params=pltpu.CompilerParams(
            collective_id=0, has_side_effects=True, vmem_limit_bytes=56 * 2**20
        ),
        name="dilated",
    )(*args)
    return tuple(o.reshape(HEADS * E, N) for o in outs)


def solution(mesh):
    spec = P("head", "seq")
    return jax.shard_map(
        per_device, mesh=mesh, in_specs=(spec,) * 4, out_specs=(spec,) * 4, check_vma=False
    )
```

profile of v0, /device:TPU:2, one launch (start us, length us, event | category | flops | bytes accessed | tf_op | source)
XLA Modules:
  0.0 51.8 jit_solution(13408431163608801499)
XLA Ops:
  0.6 46.8 %dilated.1 = (bf16[3,64,512]{2,1,0:T(8,128)(2,1)}, bf16[3,64,512]{2,1,0:T(8,128)(2,1)}, bf16[3,64,512]{2,1,0:T(8,128)(2,1)}, bf16[3,64,512]{2,1,0:T(8,128)(2,1)}) custom-call(bf16[3,64,512]{2,1,0:T(8,128)(2,1)} %bitcast.12, bf16[3,64,512]{2,1,0:T(8,128)(2,1)} %bitcast.13, bf16[3,64,512]{2,1,0:T(8,128)(2,1)} %bitcast.14, bf16[3,64,512]{2,1,0:T(8,128)(2,1)} %bitcast.15), custom_call_target="tpu_custom_call" | custom-call | tf_op jit(solution)/shard_map/dilated/pallas_call | solution.py:406
  47.4 0.0 copy-start.2
  47.4 1.7 %copy.12 = bf16[192,512]{1,0:T(8,128)(2,1)} copy(bf16[192,512]{1,0:T(8,128)(2,1)} %bitcast.11) | data formatting | bytes 393216
  49.1 0.0 copy-done.2
  49.1 0.0 copy-start.1
  49.1 0.7 %copy.13 = bf16[192,512]{1,0:T(8,128)(2,1)} copy(bf16[192,512]{1,0:T(8,128)(2,1)S(1)} %bitcast.10) | data formatting | bytes 393216
  49.8 0.3 copy-done.1
  50.1 0.0 copy-start
  50.1 0.7 %copy.14 = bf16[192,512]{1,0:T(8,128)(2,1)} copy(bf16[192,512]{1,0:T(8,128)(2,1)S(1)} %bitcast.9) | data formatting | bytes 393216
  50.8 0.3 copy-done
  51.1 0.7 %copy.15 = bf16[192,512]{1,0:T(8,128)(2,1)} copy(bf16[192,512]{1,0:T(8,128)(2,1)S(1)} %bitcast.8) | data formatting | bytes 393216
Async XLA Ops:
  47.4 1.7 %copy-start.2 = (bf16[3,64,512]{2,1,0:T(8,128)(2,1)S(1)}, bf16[3,64,512]{2,1,0:T(8,128)(2,1)}, u32[]{:S(2)}) copy-start(bf16[3,64,512]{2,1,0:T(8,128)(2,1)} %get-tuple-element.9) | copy-start | bytes 589828
  49.1 1.0 %copy-start.1 = (bf16[3,64,512]{2,1,0:T(8,128)(2,1)S(1)}, bf16[3,64,512]{2,1,0:T(8,128)(2,1)}, u32[]{:S(2)}) copy-start(bf16[3,64,512]{2,1,0:T(8,128)(2,1)} %get-tuple-element.10) | copy-start | bytes 589828
  50.1 1.0 %copy-start = (bf16[3,64,512]{2,1,0:T(8,128)(2,1)S(1)}, bf16[3,64,512]{2,1,0:T(8,128)(2,1)}, u32[]{:S(2)}) copy-start(bf16[3,64,512]{2,1,0:T(8,128)(2,1)} %get-tuple-element.11) | copy-start | bytes 589828
where the time goes:
time: 52.4 us; the launch traced here: 51.8 us
  Pallas kernels  46.8 us (89%)
  local copies, waits for them, and re-layouts  4.33 us (8%)
  between operations  0.65 us (1%)
    pallas_call x1, Pallas kernels, per_device(): pl.pallas_call(body, out_shape=[jax.ShapeDtypeStruct(shape, BF16)] * 4, i...  46.8 us
    unnamed x10, local copies, waits for them, and re-layouts  4.33 us

commit v1 on v0

v1 whole, which is shorter than its diff:
```python
import math

import jax
import jax.numpy as jnp
from jax import lax
from jax.experimental import pallas as pl
from jax.experimental.pallas import tpu as pltpu
from jax.sharding import PartitionSpec as P

E = 64
HEADS = 3
N = 512
W = HEADS * 128
F32 = jnp.float32
BF16 = jnp.bfloat16
NEG = -1e30
SCALE2 = math.log2(math.e) / math.sqrt(E)

ROWS = 1536
Y_AT, Y_ROWS = {1: 0, 2: 256, 3: 384}, {1: 256, 2: 128, 3: 128}
X_AT, X_ROWS = {4: 512, 8: 768, 12: 896}, {4: 64, 8: 32, 12: 32}
S5, S6 = 1024, 1280


def slot_at(d):
    return X_AT[d // 4 * 4] + X_ROWS[d // 4 * 4] * (d % 4)


def nn(a, b):
    return lax.dot_general(a, b, (((1,), (0,)), ((), ())), preferred_element_type=F32)


def nt(a, b):
    return lax.dot_general(a, b, (((1,), (1,)), ((), ())), preferred_element_type=F32)


def level_of(index):
    level = jnp.zeros(index.shape, jnp.int32)
    for bound in (8, 16, 32, 64, 128, 256):
        level = level + (index < bound).astype(jnp.int32)
    return level


def body(
    q_hbm, k_hbm, v_hbm, c_hbm, out,
    xin, pt, own, d6, qc, xp, rq, rc, bias0, bias1, bias2,
    e0, dp0, e1, dp1, e2, dp2, num, nums, dqa, early,
    rk, rkt, t32, t48, gsend, yacc, xacc, pacc, oacc,
    rx0, rx12, r3, rz5, rz6, ry, pz, ryz, rzz,
    in_sem, send_sem, recv_sem,
):
    me = lax.axis_index("seq")
    head0 = lax.axis_index("head") * HEADS
    z, x, y = lax.div(me, 16), lax.rem(lax.div(me, 4), 4), lax.rem(me, 4)

    def flipped(v, bits):
        if bits == 0:
            return v
        if bits == 1:
            return v + 1 - 2 * lax.rem(v, 2)
        if bits == 2:
            return lax.rem(v + 2, 4)
        return 3 - v

    peer = {e: flipped(z, e // 16) * 16 + flipped(x, e // 4 % 4) * 4 + flipped(y, e % 4)
            for e in (1, 2, 3, 4, 8, 12, 16, 32, 48)}

    loads = []
    for at, src in enumerate((k_hbm, v_hbm, q_hbm, c_hbm)):
        load = pltpu.make_async_copy(src, xin.at[:, pl.ds(64 * at, 64), :], in_sem.at[at])
        load.start()
        loads.append(load)
    barrier = pltpu.get_barrier_semaphore()
    for e in peer:
        pl.semaphore_signal(
            barrier, inc=1, device_id={"seq": peer[e]}, device_id_type=pl.DeviceIdType.MESH
        )

    copies, landed = {}, set()

    def send(key, src, dst, e):
        at = len(copies)
        copies[key] = pltpu.make_async_remote_copy(
            src_ref=src,
            dst_ref=dst,
            send_sem=send_sem.at[at],
            recv_sem=recv_sem.at[at],
            device_id={"seq": peer[e]},
            device_id_type=pl.DeviceIdType.MESH,
        )
        copies[key].start()

    def need(*keys):
        for key in keys:
            if key not in landed:
                copies[key].wait_recv()
                landed.add(key)

    def move(key, e, src, a, dst, b, n):
        send(key, src.at[a : a + n], dst.at[b : b + n], e)

    def head_lanes(h):
        return slice(128 * h, 128 * h + 128)

    place = lax.broadcasted_iota(jnp.int32, (N, 128), 0)
    lane = lax.broadcasted_iota(jnp.int32, (8, 128), 1)
    u = 64 * place
    for bits in range(4, 10):
        u = jnp.where(place >= 1 << (bits - 1), ((2 * place + 1) << (9 - bits)) & (N - 1), u)
    for h in range(HEADS):
        for t in range(4):
            tile = (lane + (128 * t + N) - (head0 + h)) & (N - 1)
            hot = u == jnp.broadcast_to(tile[0:1], (N, 128))
            pt[h, :, 128 * t : 128 * t + 128] = jnp.where(hot, 1.0, 0.0).astype(BF16)

    for load in loads[0:2]:
        load.wait()
    for h in range(HEADS):
        rows = nt(pt[h], xin[h, 0:128, :])
        own[:, head_lanes(h)] = rows.astype(BF16)
        d6[:, head_lanes(h)] = jnp.concatenate([rows[0:8]] * 2, axis=0).astype(BF16)

    pl.semaphore_wait(barrier, len(peer))
    move("x4_0", 4, own, 0, rk, slot_at(4), 64)
    move("ya1", 1, own, 0, rk, Y_AT[1], 64)
    send("z32", d6, t32, 32)
    send("z48", d6, t48, 48)
    move("ya3", 3, own, 0, rk, Y_AT[3], 64)
    move("x8_0", 8, own, 0, rk, slot_at(8), 32)
    move("ya2", 2, own, 0, rk, Y_AT[2], 64)
    move("x12_0", 12, own, 0, rk, slot_at(12), 32)
    move("zl0", 16, own, 0, rk, S5, 16)

    for load in loads[2:4]:
        load.wait()
    low = lax.broadcasted_iota(jnp.int32, (N, 128), 1) < E
    zero = jnp.zeros((E, N), BF16)
    for h in range(HEADS):
        right = nt(pt[h], xin[h, 128:256, :])
        qc[h, 0:N, :] = jnp.where(low, right, 0.0).astype(BF16)
        qc[h, N : 2 * N, :] = jnp.where(low, 0.0, right).astype(BF16)
        cols = nt(xin[h], pt[h]).astype(BF16)
        xp[h] = cols
        rq[h, 0:E, :] = cols[128:192]
        rq[h, E:128, :] = zero
        rc[h, 0:E, :] = zero
        rc[h, E:128, :] = cols[192:256]

    def fill_bias(ref, at, rows, lanes, key_place, group):
        lq = level_of(lax.broadcasted_iota(jnp.int32, (rows, lanes), 1))
        mult = jnp.minimum(lq, level_of(key_place)) - (group - 1)
        value = jnp.where(mult > 0, jnp.log2(jnp.maximum(mult, 1).astype(F32)), NEG)
        ref[at : at + rows, :] = value

    wide = lax.broadcasted_iota(jnp.int32, (256, 256), 0)
    r256 = lax.broadcasted_iota(jnp.int32, (256, 128), 0)
    fill_bias(bias0, 0, 256, 256, wide, 0)

    def forward(score, values):
        peak = jnp.max(score, axis=0, keepdims=True)
        expo = jnp.exp2(score - peak)
        total = jnp.sum(expo, axis=0, keepdims=True)
        return peak, expo, total, nn(values, expo.astype(BF16))[E:128]

    local = [[] for _ in range(HEADS)]
    part1 = [None] * HEADS
    parts2 = [[] for _ in range(HEADS)]

    def local_forward(h):
        for t in range(2):
            qs = slice(256 * t, 256 * t + 256)
            score = nn(own[:, head_lanes(h)], rq[h, :, qs]) * SCALE2
            if t == 0:
                score = jnp.concatenate([score[0:256] + bias0[...], score[256:512]], axis=0)
            peak, expo, total, mix = forward(score, xp[h, 0:128, :])
            e0[h, :, qs] = expo
            num[h, :, qs] = mix
            local[h].append((peak, total))

    def remote_forward(h, a, b):
        ks = slice(256 + a, 256 + b)
        keys = rk[ks, head_lanes(h)]
        rkt[h, :, ks] = keys.T
        dp2[h, a:b, :] = nn(keys, rc[h, :, 0:128])
        score = nn(keys, rq[h, :, 0:128]) * SCALE2 + bias2[a:b, :]
        peak, expo, total, mix = forward(score, rkt[h, :, ks])
        e2[h, a:b, :] = expo
        at = 256 + 128 * len(parts2[h])
        nums[h, :, at : at + 128] = mix
        parts2[h].append((peak, total, at, a, b))

    local_forward(0)

    need("z32", "z48")
    rk[S6 : S6 + 16, :] = jnp.concatenate(
        [t32[...].astype(F32)[0:8], t48[...].astype(F32)[8:16]], axis=0
    ).astype(BF16)
    for e in (1, 2, 3, 4, 8, 12):
        move(f"p{e}", e, rk, S6, rk, S6 + 16 * e, 16)
    for b in (1, 2):
        need(f"ya{b}")
        for e in (4, 8, 12):
            move(f"x{e}_{b}", e, rk, Y_AT[b], rk, slot_at(e + b), X_ROWS[e])
    for e in (4, 12, 8):
        need(f"x{e}_0")
        move(f"x{e}_3", 3, rk, slot_at(e), rk, slot_at(e + 3), X_ROWS[e])
    move("yb1", 1, own, 64, rk, Y_AT[1] + 64, 192)
    move("yb3", 3, own, 64, rk, Y_AT[3] + 64, 64)
    move("yb2", 2, own, 64, rk, Y_AT[2] + 64, 64)

    def last_z(*slots):
        for d in slots:
            src = Y_AT[d] if d < 4 else slot_at(d)
            move(f"zl{d}", 16, rk, src, rk, S5 + 16 * d, 16)

    need("ya3")
    last_z(1, 2, 3, 4, 8, 12)

    local_forward(1)
    need("p1", "p2", "p3")
    for e in (4, 8, 12):
        move(f"pp{e}", e, rk, S6 + 16, rk, S6 + 16 * e + 16, 48)
    for e in (4, 12, 8):
        need(f"x{e}_1")
        last_z(e + 1)
    for e in (4, 12, 8):
        need(f"x{e}_2")
        last_z(e + 2)
    for e in (4, 12, 8):
        need(f"x{e}_3")
        last_z(e + 3)

    local_forward(2)
    fill_bias(bias2, 256, 256, 128, r256 & 63, 3)
    fill_bias(bias2, 512, 256, 128, r256 & 31, 4)
    fill_bias(bias2, 768, 256, 128, r256 & 15, 5)
    fill_bias(bias2, 1024, 256, 128, r256 & 7, 6)
    for h in range(HEADS):
        remote_forward(h, 256, 768)
    fill_bias(bias1, 0, 256, 256, wide, 1)
    fill_bias(bias2, 0, 256, 128, r256 & 127, 2)
    for h in range(HEADS):
        dp0[h] = nn(own[:, head_lanes(h)], rc[h])
    need("yb1", "yb2", "yb3")
    for h in range(HEADS):
        keys = rk[0:256, head_lanes(h)]
        rkt[h, :, 0:256] = keys.T
        dp1[h] = nn(keys, rc[h, :, 0:256])
        score = nn(keys, rq[h, :, 0:256]) * SCALE2 + bias1[...]
        peak, expo, total, mix = forward(score, rkt[h, :, 0:256])
        e1[h] = expo
        nums[h, :, 0:256] = mix
        part1[h] = (peak, total)
        remote_forward(h, 0, 256)
    for e in (4, 8, 12):
        need(f"p{e}", f"pp{e}")
    need(*(f"zl{d}" for d in range(16)))
    for h in range(HEADS):
        remote_forward(h, 768, 1280)

    def combine(h, lo, hi):
        t = lo // 256
        ls = slice(lo - 256 * t, hi - 256 * t)
        pieces = [(local[h][t][0][:, ls], local[h][t][1][:, ls], num[h, :, lo:hi])]
        if hi <= 256:
            pieces.append((part1[h][0][:, lo:hi], part1[h][1][:, lo:hi], nums[h, :, lo:hi]))
        if hi <= 128:
            for peak, total, at, _, _ in parts2[h]:
                pieces.append((peak, total, nums[h, :, at : at + 128]))
        top = pieces[0][0]
        for peak, _, _ in pieces[1:]:
            top = jnp.maximum(top, peak)
        factors = [jnp.exp2(peak - top) for peak, _, _ in pieces]
        inv = 1.0 / sum(f * total for f, (_, total, _) in zip(factors, pieces))
        gains = [f * inv for f in factors]
        attended = sum(g * mix for g, (_, _, mix) in zip(gains, pieces)).astype(BF16)
        cot = xp[h, 192:256, lo:hi].astype(F32)
        delta = jnp.sum(cot * attended.astype(F32), axis=0, keepdims=True)
        xp[h, 192:256, lo:hi] = attended
        return gains, delta

    def backward(h, dprob, expo, gain, delta, nq):
        probs = expo * gain
        dscore = (probs * (dprob - delta)).astype(BF16)
        both = jnp.concatenate([dscore, probs.astype(BF16)], axis=1)
        right = jnp.concatenate([qc[h, 0:nq, :], qc[h, N : N + nq, :]], axis=0)
        return dscore, nn(both, right)

    def remote_backward(h, which):
        _, _, _, a, b = parts2[h][which]
        gains, delta = first[h]
        dscore, dkv = backward(h, dp2[h, a:b, :], e2[h, a:b, :], gains[2 + which], delta, 128)
        return nn(rkt[h, :, 256 + a : 256 + b], dscore)[0:E], dkv

    first = [combine(h, 0, 128) for h in range(HEADS)]
    for h in range(HEADS):
        hs = head_lanes(h)
        dq, dkv = remote_backward(h, 0)
        gsend[512:1024, hs] = dkv.astype(BF16)
        xacc[0:64, hs] = dkv[0:64]
        xacc[64:96, hs] = dkv[256:288]
        xacc[96:128, hs] = dkv[384:416]
        dqz, dkv = remote_backward(h, 2)
        gsend[1024:1536, hs] = dkv.astype(BF16)
        pacc[0:64, hs] = dkv[0:64]
        pacc[64:128, hs] = dkv[256:320]
        dqa[h, :, 0:128] = dq + dqz
        dqa[h, :, 128:256] = jnp.zeros((E, 128), F32)
    r3_at = {4: 0, 8: 64, 12: 96}
    for e in (4, 8, 12):
        move(f"g{e}_3", 3, gsend, slot_at(e + 3), r3, r3_at[e], X_ROWS[e])
    z_at = {4: 0, 8: 64, 12: 128}
    x12_at = {4: 0, 8: 128, 12: 192}
    for e in (4, 8, 12):
        move(f"gp5{e}", e, gsend, S5 + 16 * e, rz5, z_at[e], 64)
        move(f"gp6{e}", e, gsend, S6 + 16 * e, rz6, z_at[e], 64)
    for e in (4, 8, 12):
        move(f"g{e}_12", e, gsend, slot_at(e + 1), rx12, x12_at[e], 2 * X_ROWS[e])

    second = [combine(h, 128, 256) for h in range(HEADS)]
    third = [combine(h, 256, 512) for h in range(HEADS)]
    delta_all = []
    for h in range(HEADS):
        hs = head_lanes(h)
        delta_all.append(jnp.concatenate([first[h][1], second[h][1], third[h][1]], axis=1))
        gain = jnp.concatenate([first[h][0][1], second[h][0][1]], axis=1)
        dscore, dkv = backward(h, dp1[h], e1[h], gain, delta_all[h][:, 0:256], 256)
        dqa[h, :, 0:256] += nn(rkt[h, :, 0:256], dscore)[0:E]
        yacc[0:64, hs] = dkv[0:64]
        gsend[64:256, hs] = dkv[64:256].astype(BF16)
        dq, dkv = remote_backward(h, 1)
        dqa[h, :, 0:128] += dq
        yacc[64:128, hs] = dkv[0:64]
        gsend[320:512, hs] = dkv[64:256].astype(BF16)
    move("gy3", 3, gsend, 384, ry, 384, 128)
    move("gy1", 1, gsend, 64, ry, 64, 192)
    move("gy2", 2, gsend, 320, ry, 320, 64)

    x0_at = {4: 0, 8: 64, 12: 96}
    for e in (4, 8, 12):
        n, at = X_ROWS[e], x0_at[e]
        need(f"g{e}_3")
        total = xacc[at : at + n, :] + r3[at : at + n, :].astype(F32)
        gsend[slot_at(e) : slot_at(e) + n, :] = total.astype(BF16)
        move(f"g{e}_0", e, gsend, slot_at(e), rx0, at, n)

    def local_backward(h):
        gain = jnp.concatenate([first[h][0][0], second[h][0][0], third[h][0][0]], axis=1)
        dscore, dkv = backward(h, dp0[h], e0[h], gain, delta_all[h], N)
        oacc[:, head_lanes(h)] = dkv
        dq = nn(xp[h, 0:128, :], dscore)[0:E]
        dq = jnp.concatenate([dq[:, 0:256] + dqa[h], dq[:, 256:512]], axis=1)
        done = nn(jnp.concatenate([xp[h, 192:256, :], dq.astype(BF16)], axis=0), pt[h])
        out[0, h] = done[0:E].astype(BF16)
        out[1, h] = (done[E:128] * 0.125).astype(BF16)

    local_backward(0)

    for e in (4, 8, 12):
        need(f"gp5{e}", f"gp6{e}")
    for b in (1, 2, 3):
        bs = slice(16 * b, 16 * b + 16)
        for part, got in ((0, rz5), (1, rz6)):
            total = pacc[64 * part + 16 * b : 64 * part + 16 * b + 16, :]
            for e in (4, 8, 12):
                total = total + got[z_at[e] + 16 * b : z_at[e] + 16 * b + 16, :].astype(F32)
            at = 32 * (b - 1) + 16 * part
            pz[at : at + 16, :] = total.astype(BF16)
        move(f"gpy{b}", b, pz, 32 * (b - 1), ryz, 32 * (b - 1), 32)
    for e in (4, 8, 12):
        need(f"g{e}_12")
    for b in (1, 2):
        part = yacc[64 * (b - 1) : 64 * b, :] + rx12[64 * (b - 1) : 64 * b, :].astype(F32)
        small = rx12[96 + 32 * b : 128 + 32 * b, :].astype(F32) + rx12[
            160 + 32 * b : 192 + 32 * b, :
        ].astype(F32)
        gsend[Y_AT[b] : Y_AT[b] + 32, :] = (part[0:32] + small).astype(BF16)
        gsend[Y_AT[b] + 32 : Y_AT[b] + 64, :] = part[32:64].astype(BF16)
        move(f"gya{b}", b, gsend, Y_AT[b], ry, Y_AT[b], 64)

    local_backward(1)

    need("gpy1", "gpy2", "gpy3")
    for part, got in ((0, rz5), (1, rz6)):
        total = pacc[64 * part : 64 * part + 16, :]
        for e in (4, 8, 12):
            total = total + got[z_at[e] : z_at[e] + 16, :].astype(F32)
        for b in (0, 1, 2):
            total = total + ryz[32 * b + 16 * part : 32 * b + 16 * part + 16, :].astype(F32)
        gsend[S5 + 256 * part : S5 + 256 * part + 16, :] = total.astype(BF16)
    move("gz16", 16, gsend, S5, rzz, 0, 16)
    move("gz32", 32, gsend, S6, rzz, 16, 16)
    move("gz48", 48, gsend, S6, rzz, 32, 16)

    local_backward(2)

    need("gy1", "gy2", "gy3")
    for h in range(HEADS):
        hs = head_lanes(h)
        b256 = oacc[128:256, hs] + ry[128:256, hs].astype(F32)
        whole = jnp.concatenate([b256, oacc[256:512, hs]], axis=0)
        early[h] = nn(whole.T.astype(BF16), pt[h, 128:512, :])
        b128 = oacc[64:128, hs]
        for b in (1, 2, 3):
            b128 = b128 + ry[Y_AT[b] + 64 : Y_AT[b] + 128, hs].astype(F32)
        oacc[64:128, hs] = b128

    need("g4_0", "g8_0", "g12_0", "gya1", "gya2", "gz16", "gz32", "gz48")
    for h in range(HEADS):
        hs = head_lanes(h)
        a = oacc[0:64, hs] + rx0[0:64, hs].astype(F32)
        for b in (1, 2, 3):
            a = a + ry[Y_AT[b] : Y_AT[b] + 64, hs].astype(F32)
        a32 = a[0:32] + rx0[64:96, hs].astype(F32) + rx0[96:128, hs].astype(F32)
        a16 = a32[0:16] + rzz[0:16, hs].astype(F32)
        a8 = a16[0:8] + rzz[16:32, hs].astype(F32)[0:8] + rzz[32:48, hs].astype(F32)[8:16]
        whole = jnp.concatenate([a8, a16[8:16], a32[16:32], a[32:64], oacc[64:128, hs]], axis=0)
        done = early[h] + nn(whole.T.astype(BF16), pt[h, 0:128, :])
        out[2, h] = (done[0:E] * 0.125).astype(BF16)
        out[3, h] = done[E:128].astype(BF16)
    for copy in copies.values():
        copy.wait_send()


def hand_out(res, o_hbm, gq_hbm, gk_hbm, gv_hbm, sem):
    moves = [
        pltpu.make_async_copy(res.at[at], dst, sem.at[at])
        for at, dst in enumerate((o_hbm, gq_hbm, gk_hbm, gv_hbm))
    ]
    for move in moves:
        move.start()
    for move in moves:
        move.wait()


COPIES = 72


def per_device(tile_query, tile_key, tile_value, out_cotangent):
    shape = (HEADS, E, N)
    args = [a.reshape(shape) for a in (tile_query, tile_key, tile_value, out_cotangent)]
    vm = pltpu.VMEM
    anywhere = pl.BlockSpec(memory_space=pl.ANY)
    res = pl.pallas_call(
        body,
        out_shape=jax.ShapeDtypeStruct((4, *shape), BF16),
        in_specs=[pl.BlockSpec(memory_space=pltpu.HBM)] * 4,
        out_specs=pl.BlockSpec(memory_space=pltpu.VMEM),
        scratch_shapes=[
            vm((HEADS, 256, N), BF16),
            vm((HEADS, N, N), BF16),
            vm((N, W), BF16),
            vm((16, W), BF16),
            vm((HEADS, 2 * N, 128), BF16),
            vm((HEADS, 256, N), BF16),
            vm((HEADS, 128, N), BF16),
            vm((HEADS, 128, N), BF16),
            vm((256, 256), F32),
            vm((256, 256), F32),
            vm((1280, 128), F32),
            vm((HEADS, N, N), F32),
            vm((HEADS, N, N), F32),
            vm((HEADS, 256, 256), F32),
            vm((HEADS, 256, 256), F32),
            vm((HEADS, 1280, 128), F32),
            vm((HEADS, 1280, 128), F32),
            vm((HEADS, E, N), F32),
            vm((HEADS, E, 640), F32),
            vm((HEADS, E, 256), F32),
            vm((HEADS, 128, N), F32),
            vm((ROWS, W), BF16),
            vm((HEADS, 128, ROWS), BF16),
            vm((16, W), BF16),
            vm((16, W), BF16),
            vm((ROWS, W), BF16),
            vm((128, W), F32),
            vm((128, W), F32),
            vm((128, W), F32),
            vm((N, W), F32),
            vm((128, W), BF16),
            vm((256, W), BF16),
            vm((128, W), BF16),
            vm((192, W), BF16),
            vm((192, W), BF16),
            vm((512, W), BF16),
            vm((96, W), BF16),
            vm((96, W), BF16),
            vm((48, W), BF16),
            pltpu.SemaphoreType.DMA((4,)),
            pltpu.SemaphoreType.DMA((COPIES,)),
            pltpu.SemaphoreType.DMA((COPIES,)),
        ],
        compiler_params=pltpu.CompilerParams(
            collective_id=0, has_side_effects=True, vmem_limit_bytes=44 * 2**20
        ),
        name="dilated",
    )(*args)
    outs = pl.pallas_call(
        hand_out,
        out_shape=[jax.ShapeDtypeStruct((HEADS * E, N), BF16)] * 4,
        in_specs=[anywhere],
        out_specs=[anywhere] * 4,
        scratch_shapes=[pltpu.SemaphoreType.DMA((4,))],
        compiler_params=pltpu.CompilerParams(vmem_limit_bytes=2**20),
        name="outputs",
    )(res.reshape(4, HEADS * E, N))
    return tuple(outs)


def solution(mesh):
    spec = P("head", "seq")
    return jax.shard_map(
        per_device, mesh=mesh, in_specs=(spec,) * 4, out_specs=(spec,) * 4, check_vma=False
    )
```

time: 52.4 us -> 43.1 us (0.82)
  Pallas kernels: 46.8 us -> 38.2 us
  local copies, waits for them, and re-layouts: 4.33 us -> 3.7 us
    pallas_call x1 -> x2, Pallas kernels: 46.8 us -> 38.2 us  [the longest x1 37.3 us: per_device(): pl.pallas_call(body, out_shape=jax.ShapeDtypeStruct((4, *shape), BF16), i...]
    unnamed x10 -> x8, local copies, waits for them, and re-layouts: 4.33 us -> 3.7 us
where the time goes in v1:
time: 43.1 us; the launch traced here: 42.6 us
  Pallas kernels  38.2 us (89%)
  local copies, waits for them, and re-layouts  3.7 us (9%)
  between operations  0.65 us (2%)
    pallas_call x1, Pallas kernels, per_device(): pl.pallas_call(body, out_shape=jax.ShapeDtypeStruct((4, *shape), BF16), i...  37.3 us
    unnamed x8, local copies, waits for them, and re-layouts  3.7 us
    pallas_call x1, Pallas kernels, per_device(): pl.pallas_call(hand_out, out_shape=[jax.ShapeDtypeStruct((HEADS * E, N),...  0.91 us

profile of v1, /device:TPU:2, one launch (start us, length us, event | category | flops | bytes accessed | tf_op | source)
XLA Modules:
  0.0 42.6 jit_solution(4079646715568916321)
XLA Ops:
  0.6 0.0 copy-start
  0.6 0.9 %copy-done = bf16[192,512]{1,0:T(8,128)(2,1)S(1)} copy-done((bf16[192,512]{1,0:T(8,128)(2,1)S(1)}, bf16[192,512]{1,0:T(8,128)(2,1)}, u32[]{:S(2)}) %copy-start) | copy-done | bytes 196632
  1.6 0.0 copy-start.1
  1.6 0.9 %copy-done.1 = bf16[192,512]{1,0:T(8,128)(2,1)S(1)} copy-done((bf16[192,512]{1,0:T(8,128)(2,1)S(1)}, bf16[192,512]{1,0:T(8,128)(2,1)}, u32[]{:S(2)}) %copy-start.1) | copy-done | bytes 196632
  2.5 0.0 copy-start.2
  2.5 0.9 %copy-done.2 = bf16[192,512]{1,0:T(8,128)(2,1)S(1)} copy-done((bf16[192,512]{1,0:T(8,128)(2,1)S(1)}, bf16[192,512]{1,0:T(8,128)(2,1)}, u32[]{:S(2)}) %copy-start.2) | copy-done | bytes 196632
  3.4 0.0 copy-start.3
  3.4 0.9 %copy-done.3 = bf16[192,512]{1,0:T(8,128)(2,1)S(1)} copy-done((bf16[192,512]{1,0:T(8,128)(2,1)S(1)}, bf16[192,512]{1,0:T(8,128)(2,1)}, u32[]{:S(2)}) %copy-start.3) | copy-done | bytes 196632
  4.3 37.3 %dilated.1 = bf16[4,3,64,512]{3,2,1,0:T(8,128)(2,1)S(1)} custom-call(bf16[3,64,512]{2,1,0:T(8,128)(2,1)S(1)} %bitcast.6, bf16[3,64,512]{2,1,0:T(8,128)(2,1)S(1)} %bitcast.7, bf16[3,64,512]{2,1,0:T(8,128)(2,1)S(1)} %bitcast.8, bf16[3,64,512]{2,1,0:T(8,128)(2,1)S(1)} %bitcast.9), custom_call_target="tpu_custom_call" | custom-call | tf_op jit(solution)/shard_map/dilated/pallas_call | solution.py:444
  41.7 0.9 %outputs.1 = (bf16[192,512]{1,0:T(8,128)(2,1)}, bf16[192,512]{1,0:T(8,128)(2,1)}, bf16[192,512]{1,0:T(8,128)(2,1)}, bf16[192,512]{1,0:T(8,128)(2,1)}) custom-call(bf16[4,192,512]{2,1,0:T(8,128)(2,1)S(1)} %bitcast.5), custom_call_target="tpu_custom_call" | custom-call | tf_op jit(solution)/shard_map/outputs/pallas_call | solution.py:498
Async XLA Ops:
  0.6 0.9 %copy-start = (bf16[192,512]{1,0:T(8,128)(2,1)S(1)}, bf16[192,512]{1,0:T(8,128)(2,1)}, u32[]{:S(2)}) copy-start(bf16[192,512]{1,0:T(8,128)(2,1)} %param.4) | copy-start | bytes 589828
  1.6 0.9 %copy-start.1 = (bf16[192,512]{1,0:T(8,128)(2,1)S(1)}, bf16[192,512]{1,0:T(8,128)(2,1)}, u32[]{:S(2)}) copy-start(bf16[192,512]{1,0:T(8,128)(2,1)} %param.5) | copy-start | bytes 589828
  2.5 0.9 %copy-start.2 = (bf16[192,512]{1,0:T(8,128)(2,1)S(1)}, bf16[192,512]{1,0:T(8,128)(2,1)}, u32[]{:S(2)}) copy-start(bf16[192,512]{1,0:T(8,128)(2,1)} %param.6) | copy-start | bytes 589828
  3.4 0.9 %copy-start.3 = (bf16[192,512]{1,0:T(8,128)(2,1)S(1)}, bf16[192,512]{1,0:T(8,128)(2,1)}, u32[]{:S(2)}) copy-start(bf16[192,512]{1,0:T(8,128)(2,1)} %param.7) | copy-start | bytes 589828

commit v2 on v1

--- a/solution.py
+++ b/solution.py
@@ -42,12 +42,13 @@
 
 
 def body(
-    q_hbm, k_hbm, v_hbm, c_hbm, out,
+    q_hbm, k_hbm, v_hbm, c_hbm, out_hbm,
+    out,
     xin, pt, own, d6, qc, xp, rq, rc, bias0, bias1, bias2,
     e0, dp0, e1, dp1, e2, dp2, num, nums, dqa, early,
     rk, rkt, t32, t48, gsend, yacc, xacc, pacc, oacc,
     rx0, rx12, r3, rz5, rz6, ry, pz, ryz, rzz,
-    in_sem, send_sem, recv_sem,
+    in_sem, out_sem, send_sem, recv_sem,
 ):
     me = lax.axis_index("seq")
     head0 = lax.axis_index("head") * HEADS
@@ -394,6 +395,9 @@
 
     local_backward(2)
 
+    stores = [pltpu.make_async_copy(out.at[0:2], out_hbm.at[0:2], out_sem.at[0])]
+    stores[0].start()
+
     need("gy1", "gy2", "gy3")
     for h in range(HEADS):
         hs = head_lanes(h)
@@ -418,19 +422,25 @@
         done = early[h] + nn(whole.T.astype(BF16), pt[h, 0:128, :])
         out[2, h] = (done[0:E] * 0.125).astype(BF16)
         out[3, h] = done[E:128].astype(BF16)
+    stores.append(pltpu.make_async_copy(out.at[2:4], out_hbm.at[2:4], out_sem.at[1]))
+    stores[1].start()
     for copy in copies.values():
         copy.wait_send()
-
-
-def hand_out(res, o_hbm, gq_hbm, gk_hbm, gv_hbm, sem):
-    moves = [
-        pltpu.make_async_copy(res.at[at], dst, sem.at[at])
-        for at, dst in enumerate((o_hbm, gq_hbm, gk_hbm, gv_hbm))
-    ]
-    for move in moves:
-        move.start()
-    for move in moves:
-        move.wait()
+    for store in stores:
+        store.wait()
+
+
+def hand_out(res, o_hbm, gq_hbm, gk_hbm, gv_hbm, held, in_sem, out_sem):
+    outs = (o_hbm, gq_hbm, gk_hbm, gv_hbm)
+    loads = [pltpu.make_async_copy(res.at[i], held.at[i], in_sem.at[i]) for i in range(4)]
+    stores = [pltpu.make_async_copy(held.at[i], outs[i], out_sem.at[i]) for i in range(4)]
+    for load in loads:
+        load.start()
+    for load, store in zip(loads, stores):
+        load.wait()
+        store.start()
+    for store in stores:
+        store.wait()
 
 
 COPIES = 72
@@ -444,9 +454,10 @@
     res = pl.pallas_call(
         body,
         out_shape=jax.ShapeDtypeStruct((4, *shape), BF16),
-        in_specs=[pl.BlockSpec(memory_space=pltpu.HBM)] * 4,
-        out_specs=pl.BlockSpec(memory_space=pltpu.VMEM),
+        in_specs=[anywhere] * 4,
+        out_specs=anywhere,
         scratch_shapes=[
+            vm((4, *shape), BF16),
             vm((HEADS, 256, N), BF16),
             vm((HEADS, N, N), BF16),
             vm((N, W), BF16),
@@ -487,11 +498,12 @@
             vm((96, W), BF16),
             vm((48, W), BF16),
             pltpu.SemaphoreType.DMA((4,)),
+            pltpu.SemaphoreType.DMA((2,)),
             pltpu.SemaphoreType.DMA((COPIES,)),
             pltpu.SemaphoreType.DMA((COPIES,)),
         ],
         compiler_params=pltpu.CompilerParams(
-            collective_id=0, has_side_effects=True, vmem_limit_bytes=44 * 2**20
+            collective_id=0, has_side_effects=True, vmem_limit_bytes=62 * 2**20
         ),
         name="dilated",
     )(*args)
@@ -500,8 +512,12 @@
         out_shape=[jax.ShapeDtypeStruct((HEADS * E, N), BF16)] * 4,
         in_specs=[anywhere],
         out_specs=[anywhere] * 4,
-        scratch_shapes=[pltpu.SemaphoreType.DMA((4,))],
-        compiler_params=pltpu.CompilerParams(vmem_limit_bytes=2**20),
+        scratch_shapes=[
+            vm((4, HEADS * E, N), BF16),
+            pltpu.SemaphoreType.DMA((4,)),
+            pltpu.SemaphoreType.DMA((4,)),
+        ],
+        compiler_params=pltpu.CompilerParams(vmem_limit_bytes=62 * 2**20),
         name="outputs",
     )(res.reshape(4, HEADS * E, N))
     return tuple(outs)

time: 43.1 us -> 41.4 us (0.961); the launches traced: 42.6 us -> 41.3 us
  local copies, waits for them, and re-layouts: 3.7 us -> 0 us
  Pallas kernels: 38.2 us -> 40.7 us
    unnamed x8 -> x0, local copies, waits for them, and re-layouts: 3.7 us -> none
    pallas_call x1, Pallas kernels: 37.3 us -> 38.7 us  [per_device(): pl.pallas_call(body, out_shape=jax.ShapeDtypeStruct((4, *shape), BF16), i...]
    pallas_call x1, Pallas kernels: 0.91 us -> 1.97 us  [per_device(): pl.pallas_call(hand_out, out_shape=[jax.ShapeDtypeStruct((HEADS * E, N),...]
where the time goes in v2:
time: 41.4 us; the launch traced here: 41.3 us
  Pallas kernels  40.7 us (98%)
  between operations  0.64 us (2%)
    pallas_call x1, Pallas kernels, per_device(): pl.pallas_call(body, out_shape=jax.ShapeDtypeStruct((4, *shape), BF16), i...  38.7 us
    pallas_call x1, Pallas kernels, per_device(): pl.pallas_call(hand_out, out_shape=[jax.ShapeDtypeStruct((HEADS * E, N),...  1.97 us

profile of v2, /device:TPU:2, one launch (start us, length us, event | category | flops | bytes accessed | tf_op | source)
XLA Modules:
  0.0 41.3 jit_solution(6319137199573962954)
XLA Ops:
  0.6 38.7 %dilated.1 = bf16[4,3,64,512]{3,2,1,0:T(8,128)(2,1)} custom-call(bf16[3,64,512]{2,1,0:T(8,128)(2,1)} %bitcast.6, bf16[3,64,512]{2,1,0:T(8,128)(2,1)} %bitcast.7, bf16[3,64,512]{2,1,0:T(8,128)(2,1)} %bitcast.8, bf16[3,64,512]{2,1,0:T(8,128)(2,1)} %bitcast.9), custom_call_target="tpu_custom_call" | custom-call | tf_op jit(solution)/shard_map/dilated/pallas_call | solution.py:454
  39.3 2.0 %outputs.1 = (bf16[192,512]{1,0:T(8,128)(2,1)}, bf16[192,512]{1,0:T(8,128)(2,1)}, bf16[192,512]{1,0:T(8,128)(2,1)}, bf16[192,512]{1,0:T(8,128)(2,1)}) custom-call(bf16[4,192,512]{2,1,0:T(8,128)(2,1)} %bitcast.5), custom_call_target="tpu_custom_call" | custom-call | tf_op jit(solution)/shard_map/outputs/pallas_call | solution.py:510

commit v3 on v1

--- a/solution.py
+++ b/solution.py
@@ -254,9 +254,11 @@
         remote_forward(h, 0, 256)
     for e in (4, 8, 12):
         need(f"p{e}", f"pp{e}")
+    for h in range(HEADS):
+        remote_forward(h, 1024, 1280)
     need(*(f"zl{d}" for d in range(16)))
     for h in range(HEADS):
-        remote_forward(h, 768, 1280)
+        remote_forward(h, 768, 1024)
 
     def combine(h, lo, hi):
         t = lo // 256
@@ -290,30 +292,33 @@
         _, _, _, a, b = parts2[h][which]
         gains, delta = first[h]
         dscore, dkv = backward(h, dp2[h, a:b, :], e2[h, a:b, :], gains[2 + which], delta, 128)
-        return nn(rkt[h, :, 256 + a : 256 + b], dscore)[0:E], dkv
+        return dkv, dscore, rkt[h, :, 256 + a : 256 + b]
 
     first = [combine(h, 0, 128) for h in range(HEADS)]
+    z_at = {4: 0, 8: 64, 12: 128}
+    queries = [[] for _ in range(HEADS)]
     for h in range(HEADS):
         hs = head_lanes(h)
-        dq, dkv = remote_backward(h, 0)
+        for which, at, kept in ((3, S5, 0), (2, S6, 64)):
+            dkv, *rest = remote_backward(h, which)
+            queries[h].append(rest)
+            gsend[at : at + 256, hs] = dkv.astype(BF16)
+            pacc[kept : kept + 64, hs] = dkv[0:64]
+    for e in (4, 8, 12):
+        move(f"gp5{e}", e, gsend, S5 + 16 * e, rz5, z_at[e], 64)
+        move(f"gp6{e}", e, gsend, S6 + 16 * e, rz6, z_at[e], 64)
+    r3_at = {4: 0, 8: 64, 12: 96}
+    x12_at = {4: 0, 8: 128, 12: 192}
+    for h in range(HEADS):
+        hs = head_lanes(h)
+        dkv, *rest = remote_backward(h, 0)
+        queries[h].append(rest)
         gsend[512:1024, hs] = dkv.astype(BF16)
         xacc[0:64, hs] = dkv[0:64]
         xacc[64:96, hs] = dkv[256:288]
         xacc[96:128, hs] = dkv[384:416]
-        dqz, dkv = remote_backward(h, 2)
-        gsend[1024:1536, hs] = dkv.astype(BF16)
-        pacc[0:64, hs] = dkv[0:64]
-        pacc[64:128, hs] = dkv[256:320]
-        dqa[h, :, 0:128] = dq + dqz
-        dqa[h, :, 128:256] = jnp.zeros((E, 128), F32)
-    r3_at = {4: 0, 8: 64, 12: 96}
     for e in (4, 8, 12):
         move(f"g{e}_3", 3, gsend, slot_at(e + 3), r3, r3_at[e], X_ROWS[e])
-    z_at = {4: 0, 8: 64, 12: 128}
-    x12_at = {4: 0, 8: 128, 12: 192}
-    for e in (4, 8, 12):
-        move(f"gp5{e}", e, gsend, S5 + 16 * e, rz5, z_at[e], 64)
-        move(f"gp6{e}", e, gsend, S6 + 16 * e, rz6, z_at[e], 64)
     for e in (4, 8, 12):
         move(f"g{e}_12", e, gsend, slot_at(e + 1), rx12, x12_at[e], 2 * X_ROWS[e])
 
@@ -325,11 +330,11 @@
         delta_all.append(jnp.concatenate([first[h][1], second[h][1], third[h][1]], axis=1))
         gain = jnp.concatenate([first[h][0][1], second[h][0][1]], axis=1)
         dscore, dkv = backward(h, dp1[h], e1[h], gain, delta_all[h][:, 0:256], 256)
-        dqa[h, :, 0:256] += nn(rkt[h, :, 0:256], dscore)[0:E]
+        dqa[h] = nn(rkt[h, :, 0:256], dscore)[0:E]
         yacc[0:64, hs] = dkv[0:64]
         gsend[64:256, hs] = dkv[64:256].astype(BF16)
-        dq, dkv = remote_backward(h, 1)
-        dqa[h, :, 0:128] += dq
+        dkv, *rest = remote_backward(h, 1)
+        dqa[h, :, 0:128] += sum(nn(values, ds)[0:E] for ds, values in [*queries[h], rest])
         yacc[64:128, hs] = dkv[0:64]
         gsend[320:512, hs] = dkv[64:256].astype(BF16)
     move("gy3", 3, gsend, 384, ry, 384, 128)
@@ -423,14 +428,14 @@
 
 
 def hand_out(res, o_hbm, gq_hbm, gk_hbm, gv_hbm, sem):
-    moves = [
+    stores = [
         pltpu.make_async_copy(res.at[at], dst, sem.at[at])
         for at, dst in enumerate((o_hbm, gq_hbm, gk_hbm, gv_hbm))
     ]
-    for move in moves:
-        move.start()
-    for move in moves:
-        move.wait()
+    for store in stores:
+        store.start()
+    for store in stores:
+        store.wait()
 
 
 COPIES = 72
@@ -438,13 +443,16 @@
 
 def per_device(tile_query, tile_key, tile_value, out_cotangent):
     shape = (HEADS, E, N)
-    args = [a.reshape(shape) for a in (tile_query, tile_key, tile_value, out_cotangent)]
+    args = [
+        pltpu.with_memory_space_constraint(a.reshape(shape), pltpu.HBM)
+        for a in (tile_query, tile_key, tile_value, out_cotangent)
+    ]
     vm = pltpu.VMEM
     anywhere = pl.BlockSpec(memory_space=pl.ANY)
     res = pl.pallas_call(
         body,
         out_shape=jax.ShapeDtypeStruct((4, *shape), BF16),
-        in_specs=[pl.BlockSpec(memory_space=pltpu.HBM)] * 4,
+        in_specs=[anywhere] * 4,
         out_specs=pl.BlockSpec(memory_space=pltpu.VMEM),
         scratch_shapes=[
             vm((HEADS, 256, N), BF16),
@@ -465,7 +473,7 @@
             vm((HEADS, 1280, 128), F32),
             vm((HEADS, 1280, 128), F32),
             vm((HEADS, E, N), F32),
-            vm((HEADS, E, 640), F32),
+            vm((HEADS, E, 768), F32),
             vm((HEADS, E, 256), F32),
             vm((HEADS, 128, N), F32),
             vm((ROWS, W), BF16),
@@ -500,7 +508,9 @@
         out_shape=[jax.ShapeDtypeStruct((HEADS * E, N), BF16)] * 4,
         in_specs=[anywhere],
         out_specs=[anywhere] * 4,
-        scratch_shapes=[pltpu.SemaphoreType.DMA((4,))],
+        scratch_shapes=[
+            pltpu.SemaphoreType.DMA((4,)),
+        ],
         compiler_params=pltpu.CompilerParams(vmem_limit_bytes=2**20),
         name="outputs",
     )(res.reshape(4, HEADS * E, N))

time: 43.1 us -> 39.8 us (0.923); the launches traced: 42.6 us -> 39.7 us
  local copies, waits for them, and re-layouts: 3.7 us -> 0 us
  Pallas kernels: 38.2 us -> 39.1 us
    unnamed x8 -> x0, local copies, waits for them, and re-layouts: 3.7 us -> none
    pallas_call x1, Pallas kernels: 37.3 us -> 38.2 us  [per_device(): pl.pallas_call(body, out_shape=jax.ShapeDtypeStruct((4, *shape), BF16), i...]
where the time goes in v3:
time: 39.8 us; the launch traced here: 39.7 us
  Pallas kernels  39.1 us (98%)
  between operations  0.64 us (2%)
    pallas_call x1, Pallas kernels, per_device(): pl.pallas_call(body, out_shape=jax.ShapeDtypeStruct((4, *shape), BF16), i...  38.2 us
    pallas_call x1, Pallas kernels, per_device(): pl.pallas_call(hand_out, out_shape=[jax.ShapeDtypeStruct((HEADS * E, N),...  0.91 us

profile of v3, /device:TPU:2, one launch (start us, length us, event | category | flops | bytes accessed | tf_op | source)
XLA Modules:
  0.0 39.7 jit_solution(4186136202259285375)
XLA Ops:
  0.6 38.2 %dilated.1 = bf16[4,3,64,512]{3,2,1,0:T(8,128)(2,1)S(1)} custom-call(bf16[3,64,512]{2,1,0:T(8,128)(2,1)} %bitcast.6, bf16[3,64,512]{2,1,0:T(8,128)(2,1)} %bitcast.7, bf16[3,64,512]{2,1,0:T(8,128)(2,1)} %bitcast.8, bf16[3,64,512]{2,1,0:T(8,128)(2,1)} %bitcast.9), custom_call_target="tpu_custom_call" | custom-call | tf_op jit(solution)/shard_map/dilated/pallas_call | solution.py:452
  38.8 0.9 %outputs.1 = (bf16[192,512]{1,0:T(8,128)(2,1)}, bf16[192,512]{1,0:T(8,128)(2,1)}, bf16[192,512]{1,0:T(8,128)(2,1)}, bf16[192,512]{1,0:T(8,128)(2,1)}) custom-call(bf16[4,192,512]{2,1,0:T(8,128)(2,1)S(1)} %bitcast.5), custom_call_target="tpu_custom_call" | custom-call | tf_op jit(solution)/shard_map/outputs/pallas_call | solution.py:506

commit v4 on v3

--- a/solution.py
+++ b/solution.py
@@ -44,7 +44,7 @@
 def body(
     q_hbm, k_hbm, v_hbm, c_hbm, out,
     xin, pt, own, d6, qc, xp, rq, rc, bias0, bias1, bias2,
-    e0, dp0, e1, dp1, e2, dp2, num, nums, dqa, early,
+    e0, e1, e2, dp2, num, nums, dqa, early,
     rk, rkt, t32, t48, gsend, yacc, xacc, pacc, oacc,
     rx0, rx12, r3, rz5, rz6, ry, pz, ryz, rzz,
     in_sem, send_sem, recv_sem,
@@ -102,22 +102,24 @@
     def head_lanes(h):
         return slice(128 * h, 128 * h + 128)
 
-    place = lax.broadcasted_iota(jnp.int32, (N, 128), 0)
-    lane = lax.broadcasted_iota(jnp.int32, (8, 128), 1)
-    u = 64 * place
-    for bits in range(4, 10):
-        u = jnp.where(place >= 1 << (bits - 1), ((2 * place + 1) << (9 - bits)) & (N - 1), u)
-    for h in range(HEADS):
-        for t in range(4):
-            tile = (lane + (128 * t + N) - (head0 + h)) & (N - 1)
-            hot = u == jnp.broadcast_to(tile[0:1], (N, 128))
-            pt[h, :, 128 * t : 128 * t + 128] = jnp.where(hot, 1.0, 0.0).astype(BF16)
-
+    def one_hot(lo, hi):
+        place = lax.broadcasted_iota(jnp.int32, (hi - lo, 128), 0) + lo
+        lane = lax.broadcasted_iota(jnp.int32, (8, 128), 1)
+        u = 64 * place
+        for bits in range(4, hi.bit_length()):
+            u = jnp.where(place >= 1 << (bits - 1), ((2 * place + 1) << (9 - bits)) & (N - 1), u)
+        for h in range(HEADS):
+            for t in range(4):
+                tile = (lane + (128 * t + N) - (head0 + h)) & (N - 1)
+                hot = u == jnp.broadcast_to(tile[0:1], (hi - lo, 128))
+                pt[h, lo:hi, 128 * t : 128 * t + 128] = jnp.where(hot, 1.0, 0.0).astype(BF16)
+
+    one_hot(0, 64)
     for load in loads[0:2]:
         load.wait()
     for h in range(HEADS):
-        rows = nt(pt[h], xin[h, 0:128, :])
-        own[:, head_lanes(h)] = rows.astype(BF16)
+        rows = nt(pt[h, 0:64, :], xin[h, 0:128, :])
+        own[0:64, head_lanes(h)] = rows.astype(BF16)
         d6[:, head_lanes(h)] = jnp.concatenate([rows[0:8]] * 2, axis=0).astype(BF16)
 
     pl.semaphore_wait(barrier, len(peer))
@@ -131,11 +133,13 @@
     move("x12_0", 12, own, 0, rk, slot_at(12), 32)
     move("zl0", 16, own, 0, rk, S5, 16)
 
+    one_hot(64, N)
     for load in loads[2:4]:
         load.wait()
     low = lax.broadcasted_iota(jnp.int32, (N, 128), 1) < E
     zero = jnp.zeros((E, N), BF16)
     for h in range(HEADS):
+        own[64:N, head_lanes(h)] = nt(pt[h, 64:N, :], xin[h, 0:128, :]).astype(BF16)
         right = nt(pt[h], xin[h, 128:256, :])
         qc[h, 0:N, :] = jnp.where(low, right, 0.0).astype(BF16)
         qc[h, N : 2 * N, :] = jnp.where(low, 0.0, right).astype(BF16)
@@ -166,22 +170,29 @@
     part1 = [None] * HEADS
     parts2 = [[] for _ in range(HEADS)]
 
-    def local_forward(h):
-        for t in range(2):
-            qs = slice(256 * t, 256 * t + 256)
-            score = nn(own[:, head_lanes(h)], rq[h, :, qs]) * SCALE2
-            if t == 0:
-                score = jnp.concatenate([score[0:256] + bias0[...], score[256:512]], axis=0)
-            peak, expo, total, mix = forward(score, xp[h, 0:128, :])
-            e0[h, :, qs] = expo
-            num[h, :, qs] = mix
-            local[h].append((peak, total))
+    def local_forward(h, t):
+        qs = slice(256 * t, 256 * t + 256)
+        score = nn(own[:, head_lanes(h)], rq[h, :, qs]) * SCALE2
+        if t == 0:
+            score = jnp.concatenate([score[0:256] + bias0[...], score[256:512]], axis=0)
+        peak, expo, total, mix = forward(score, xp[h, 0:128, :])
+        e0[h, :, qs] = expo
+        num[h, :, qs] = mix
+        local[h].append((peak, total))
+
+    eye = jnp.where(
+        lax.broadcasted_iota(jnp.int32, (128, 128), 0)
+        == lax.broadcasted_iota(jnp.int32, (128, 128), 1),
+        1.0,
+        0.0,
+    ).astype(BF16)
 
     def remote_forward(h, a, b):
         ks = slice(256 + a, 256 + b)
         keys = rk[ks, head_lanes(h)]
-        rkt[h, :, ks] = keys.T
-        dp2[h, a:b, :] = nn(keys, rc[h, :, 0:128])
+        rkt[h, :, ks] = nt(eye, keys).astype(BF16)
+        if a >= 256:
+            dp2[h, a - 256 : b - 256, :] = nn(keys, rc[h, :, 0:128])
         score = nn(keys, rq[h, :, 0:128]) * SCALE2 + bias2[a:b, :]
         peak, expo, total, mix = forward(score, rkt[h, :, ks])
         e2[h, a:b, :] = expo
@@ -189,7 +200,7 @@
         nums[h, :, at : at + 128] = mix
         parts2[h].append((peak, total, at, a, b))
 
-    local_forward(0)
+    local_forward(0, 0)
 
     need("z32", "z48")
     rk[S6 : S6 + 16, :] = jnp.concatenate(
@@ -216,7 +227,7 @@
     need("ya3")
     last_z(1, 2, 3, 4, 8, 12)
 
-    local_forward(1)
+    local_forward(1, 0)
     need("p1", "p2", "p3")
     for e in (4, 8, 12):
         move(f"pp{e}", e, rk, S6 + 16, rk, S6 + 16 * e + 16, 48)
@@ -230,7 +241,7 @@
         need(f"x{e}_3")
         last_z(e + 3)
 
-    local_forward(2)
+    local_forward(2, 0)
     fill_bias(bias2, 256, 256, 128, r256 & 63, 3)
     fill_bias(bias2, 512, 256, 128, r256 & 31, 4)
     fill_bias(bias2, 768, 256, 128, r256 & 15, 5)
@@ -239,13 +250,10 @@
         remote_forward(h, 256, 768)
     fill_bias(bias1, 0, 256, 256, wide, 1)
     fill_bias(bias2, 0, 256, 128, r256 & 127, 2)
-    for h in range(HEADS):
-        dp0[h] = nn(own[:, head_lanes(h)], rc[h])
     need("yb1", "yb2", "yb3")
     for h in range(HEADS):
         keys = rk[0:256, head_lanes(h)]
-        rkt[h, :, 0:256] = keys.T
-        dp1[h] = nn(keys, rc[h, :, 0:256])
+        rkt[h, :, 0:256] = nt(eye, keys).astype(BF16)
         score = nn(keys, rq[h, :, 0:256]) * SCALE2 + bias1[...]
         peak, expo, total, mix = forward(score, rkt[h, :, 0:256])
         e1[h] = expo
@@ -291,7 +299,11 @@
     def remote_backward(h, which):
         _, _, _, a, b = parts2[h][which]
         gains, delta = first[h]
-        dscore, dkv = backward(h, dp2[h, a:b, :], e2[h, a:b, :], gains[2 + which], delta, 128)
+        if a >= 256:
+            dprob = dp2[h, a - 256 : b - 256, :]
+        else:
+            dprob = nn(rk[256 + a : 256 + b, head_lanes(h)], rc[h, :, 0:128])
+        dscore, dkv = backward(h, dprob, e2[h, a:b, :], gains[2 + which], delta, 128)
         return dkv, dscore, rkt[h, :, 256 + a : 256 + b]
 
     first = [combine(h, 0, 128) for h in range(HEADS)]
@@ -323,13 +335,12 @@
         move(f"g{e}_12", e, gsend, slot_at(e + 1), rx12, x12_at[e], 2 * X_ROWS[e])
 
     second = [combine(h, 128, 256) for h in range(HEADS)]
-    third = [combine(h, 256, 512) for h in range(HEADS)]
-    delta_all = []
     for h in range(HEADS):
         hs = head_lanes(h)
-        delta_all.append(jnp.concatenate([first[h][1], second[h][1], third[h][1]], axis=1))
+        delta = jnp.concatenate([first[h][1], second[h][1]], axis=1)
         gain = jnp.concatenate([first[h][0][1], second[h][0][1]], axis=1)
-        dscore, dkv = backward(h, dp1[h], e1[h], gain, delta_all[h][:, 0:256], 256)
+        dprob = nn(rk[0:256, hs], rc[h, :, 0:256])
+        dscore, dkv = backward(h, dprob, e1[h], gain, delta, 256)
         dqa[h] = nn(rkt[h, :, 0:256], dscore)[0:E]
         yacc[0:64, hs] = dkv[0:64]
         gsend[64:256, hs] = dkv[64:256].astype(BF16)
@@ -350,8 +361,12 @@
         move(f"g{e}_0", e, gsend, slot_at(e), rx0, at, n)
 
     def local_backward(h):
-        gain = jnp.concatenate([first[h][0][0], second[h][0][0], third[h][0][0]], axis=1)
-        dscore, dkv = backward(h, dp0[h], e0[h], gain, delta_all[h], N)
+        local_forward(h, 1)
+        ranges = (first[h], second[h], combine(h, 256, 512))
+        gain = jnp.concatenate([gains[0] for gains, _ in ranges], axis=1)
+        delta = jnp.concatenate([part for _, part in ranges], axis=1)
+        dprob = nn(own[:, head_lanes(h)], rc[h])
+        dscore, dkv = backward(h, dprob, e0[h], gain, delta, N)
         oacc[:, head_lanes(h)] = dkv
         dq = nn(xp[h, 0:128, :], dscore)[0:E]
         dq = jnp.concatenate([dq[:, 0:256] + dqa[h], dq[:, 256:512]], axis=1)
@@ -467,11 +482,9 @@
             vm((256, 256), F32),
             vm((1280, 128), F32),
             vm((HEADS, N, N), F32),
-            vm((HEADS, N, N), F32),
-            vm((HEADS, 256, 256), F32),
             vm((HEADS, 256, 256), F32),
             vm((HEADS, 1280, 128), F32),
-            vm((HEADS, 1280, 128), F32),
+            vm((HEADS, 1024, 128), F32),
             vm((HEADS, E, N), F32),
             vm((HEADS, E, 768), F32),
             vm((HEADS, E, 256), F32),

time: 39.8 us -> 38.7 us (0.972)
  Pallas kernels: 39.1 us -> 37.6 us
    pallas_call x1, Pallas kernels: 38.2 us -> 36.7 us  [per_device(): pl.pallas_call(body, out_shape=jax.ShapeDtypeStruct((4, *shape), BF16), i...]
where the time goes in v4:
time: 38.7 us; the launch traced here: 38.3 us
  Pallas kernels  37.6 us (97%)
  between operations  0.64 us (2%)
    pallas_call x1, Pallas kernels, per_device(): pl.pallas_call(body, out_shape=jax.ShapeDtypeStruct((4, *shape), BF16), i...  36.7 us
    pallas_call x1, Pallas kernels, per_device(): pl.pallas_call(hand_out, out_shape=[jax.ShapeDtypeStruct((HEADS * E, N),...  0.91 us

profile of v4, /device:TPU:2, one launch (start us, length us, event | category | flops | bytes accessed | tf_op | source)
XLA Modules:
  0.0 38.3 jit_solution(8823729784235776319)
XLA Ops:
  0.6 36.7 %dilated.1 = bf16[4,3,64,512]{3,2,1,0:T(8,128)(2,1)S(1)} custom-call(bf16[3,64,512]{2,1,0:T(8,128)(2,1)} %bitcast.6, bf16[3,64,512]{2,1,0:T(8,128)(2,1)} %bitcast.7, bf16[3,64,512]{2,1,0:T(8,128)(2,1)} %bitcast.8, bf16[3,64,512]{2,1,0:T(8,128)(2,1)} %bitcast.9), custom_call_target="tpu_custom_call" | custom-call | tf_op jit(solution)/shard_map/dilated/pallas_call | solution.py:467
  37.3 0.9 %outputs.1 = (bf16[192,512]{1,0:T(8,128)(2,1)}, bf16[192,512]{1,0:T(8,128)(2,1)}, bf16[192,512]{1,0:T(8,128)(2,1)}, bf16[192,512]{1,0:T(8,128)(2,1)}) custom-call(bf16[4,192,512]{2,1,0:T(8,128)(2,1)S(1)} %bitcast.5), custom_call_target="tpu_custom_call" | custom-call | tf_op jit(solution)/shard_map/outputs/pallas_call | solution.py:519

commit v5 on v4

--- a/solution.py
+++ b/solution.py
@@ -316,7 +316,7 @@
             queries[h].append(rest)
             gsend[at : at + 256, hs] = dkv.astype(BF16)
             pacc[kept : kept + 64, hs] = dkv[0:64]
-    for e in (4, 8, 12):
+    for e in (8, 4, 12):
         move(f"gp5{e}", e, gsend, S5 + 16 * e, rz5, z_at[e], 64)
         move(f"gp6{e}", e, gsend, S6 + 16 * e, rz6, z_at[e], 64)
     r3_at = {4: 0, 8: 64, 12: 96}

time: 38.7 us -> 37.9 us (0.979)
  Pallas kernels: 37.6 us -> 37.1 us
    pallas_call x1, Pallas kernels: 36.7 us -> 36.2 us  [per_device(): pl.pallas_call(body, out_shape=jax.ShapeDtypeStruct((4, *shape), BF16), i...]
where the time goes in v5:
time: 37.9 us; the launch traced here: 37.8 us
  Pallas kernels  37.1 us (98%)
  between operations  0.64 us (2%)
    pallas_call x1, Pallas kernels, per_device(): pl.pallas_call(body, out_shape=jax.ShapeDtypeStruct((4, *shape), BF16), i...  36.2 us
    pallas_call x1, Pallas kernels, per_device(): pl.pallas_call(hand_out, out_shape=[jax.ShapeDtypeStruct((HEADS * E, N),...  0.91 us

profile of v5, /device:TPU:2, one launch (start us, length us, event | category | flops | bytes accessed | tf_op | source)
XLA Modules:
  0.0 37.8 jit_solution(8298288692293025866)
XLA Ops:
  0.6 36.2 %dilated.1 = bf16[4,3,64,512]{3,2,1,0:T(8,128)(2,1)S(1)} custom-call(bf16[3,64,512]{2,1,0:T(8,128)(2,1)} %bitcast.6, bf16[3,64,512]{2,1,0:T(8,128)(2,1)} %bitcast.7, bf16[3,64,512]{2,1,0:T(8,128)(2,1)} %bitcast.8, bf16[3,64,512]{2,1,0:T(8,128)(2,1)} %bitcast.9), custom_call_target="tpu_custom_call" | custom-call | tf_op jit(solution)/shard_map/dilated/pallas_call | solution.py:467
  36.9 0.9 %outputs.1 = (bf16[192,512]{1,0:T(8,128)(2,1)}, bf16[192,512]{1,0:T(8,128)(2,1)}, bf16[192,512]{1,0:T(8,128)(2,1)}, bf16[192,512]{1,0:T(8,128)(2,1)}) custom-call(bf16[4,192,512]{2,1,0:T(8,128)(2,1)S(1)} %bitcast.5), custom_call_target="tpu_custom_call" | custom-call | tf_op jit(solution)/shard_map/outputs/pallas_call | solution.py:519
